TPU v7x, 128 devices: a whole 4x4x4 slice. The times are simulated.
128 devices in a mesh: doc: 16 (over y, z), own: 8 (over x, core).
Axes of the slice: x: 4, y: 4, z: 4, core: 2. Of those that a mesh axis runs over, the one named last changes fastest.
Arguments:
- embeddings: bfloat16 [65536, 768], P(('doc', 'own')), may hold values from -6 to 6
- cluster_ids: int32 [65536], P(('doc', 'own')), may hold values from 0 to 50175, as said below
- keep_flags: int32 [65536], P(('doc', 'own')), may hold values 0 or 1
Outputs:
- centroids: bfloat16 [50176, 768], P(('doc', 'own'))
- scores: float32 [65536], P(('doc', 'own'))
Inputs may be any that keep to these rules, and one draw needn't show every extreme that they name: `cluster_ids`: cluster c is held by device c // 392 of the rows' order. Among the rows of one device, at most 8 name clusters held by any one device, and exactly 8 do for one device.
All inputs are finite; a program needn't handle non-finite values. No bound on the sum of `keep_flags` on one device may be relied on, other than what follows from the above.
Results may differ from a plain program's by a relative error of at most 0.0015.
Values may be sent and summed in bfloat16 or wider, within the bound.
No kernel may reach another device: no remote copies, remote signals or barrier semaphores. Data moves between devices by JAX's collectives and lax.ppermute only.
A program may use at most 64 MiB of HBM per device.

v0:
```python
import math
import jax
import jax.numpy as jnp
from jax import lax
from jax.sharding import PartitionSpec as P

CLUSTER_DEV = 392


def unit_rows(sums, width):
    inv_scale = lax.rsqrt(jnp.mean(sums * sums, axis=1, keepdims=True) + 1e-06) / math.sqrt(width)
    return (sums * inv_scale).astype(jnp.bfloat16)


def pack_rows(embeddings, slot_code, slot, slots_total):
    width = embeddings.shape[1]
    outgoing = jnp.zeros((slots_total, width), jnp.bfloat16).at[slot].set(embeddings)
    codes_out = jnp.full((slots_total,), -1, jnp.int32).at[slot].set(slot_code)
    return (outgoing, codes_out)


def body(embeddings, cluster_ids, keep_flags):
    row_count = embeddings.shape[0]
    width = embeddings.shape[1]
    grid_size = lax.axis_size(("doc", "own"))
    doc_count = lax.axis_size("doc")
    own_count = lax.axis_size("own")
    capacity = 2 * row_count // grid_size
    slots_total = grid_size * capacity
    per_device = CLUSTER_DEV
    target = cluster_ids // per_device
    local_id = cluster_ids % per_device
    hits = (target[:, None] == jnp.arange(grid_size, dtype=jnp.int32)[None, :]).astype(jnp.int32)
    position = jnp.sum(jnp.cumsum(hits, axis=0) * hits, axis=1) - 1
    slot_code = local_id + per_device * keep_flags
    row_scale = lax.rsqrt(
        jnp.mean(jnp.square(embeddings.astype(jnp.float32)), axis=1) + 1e-06
    ) / math.sqrt(width)
    slot = (target % own_count * doc_count + target // own_count) * capacity + position
    outgoing, codes_out = pack_rows(embeddings, slot_code, slot, slots_total)
    arrived, codes_in = (
        lax.all_to_all(outgoing, "own", split_axis=0, concat_axis=0, tiled=True),
        lax.all_to_all(codes_out, "own", split_axis=0, concat_axis=0, tiled=True),
    )
    slot_doc = jnp.arange(slots_total, dtype=jnp.int32) // capacity % doc_count
    valid = codes_in >= 0
    owner_index = jnp.where(valid, slot_doc * per_device + codes_in % per_device, -1)
    weight = jnp.where(valid, codes_in // per_device, 0)
    labels = jnp.arange(per_device * lax.axis_size("doc"), dtype=jnp.int32)
    table = ((labels[:, None] == owner_index[None, :]) * weight[None, :]).astype(jnp.bfloat16)
    sums = lax.psum_scatter(
        jnp.dot(table, arrived, preferred_element_type=jnp.float32),
        "doc",
        scatter_dimension=0,
        tiled=True,
    )
    centroids = unit_rows(sums, width)
    piece = lax.all_gather(centroids, "doc", axis=0, tiled=True)
    similar = jnp.dot(arrived, piece.T, preferred_element_type=jnp.float32)
    column = owner_index - jnp.int32(0)
    chosen = column[:, None] == jnp.arange(piece.shape[0], dtype=jnp.int32)[None, :]
    products = jnp.sum(jnp.where(chosen, similar, 0.0), axis=1)
    returned = lax.all_to_all(products, "own", split_axis=0, concat_axis=0, tiled=True)
    scores = returned[slot] * row_scale
    return (centroids, scores)


def solution(mesh):
    in_specs = (P(("doc", "own"), None), P(("doc", "own")), P(("doc", "own")))
    out_specs = (P(("doc", "own"), None), P(("doc", "own")))
    return jax.shard_map(body, mesh=mesh, in_specs=in_specs, out_specs=out_specs, check_vma=False)
```

profile of v0, /device:TPU:1, one launch (start us, length us, event | category | flops | bytes accessed | tf_op | source)
XLA Modules:
  0.0 299.3 jit_solution(1905121783948206056)
XLA Ops:
  7.2 0.0 copy-start.1
  7.2 0.8 fusion.25
  8.0 0.1 copy.7
  8.1 0.2 fusion.7
  8.4 0.2 fusion.6
  8.6 3.0 %scatter_custom_fusion = s32[1024]{0:T(1024)} fusion(s32[512]{0:T(512)S(1)} %compare_select_fusion, s32[512]{0:T(512)S(1)} %get-tuple-element.4, s32[]{:T(128)} %constant.95.clone.1), kind=kCustom, calls=%fused_computation.66 | custom fusion | bytes 4100 | tf_op jit(solution)/shard_map/scatter | solution.py:18
  11.7 5.8 %all-to-all-start = ((s32[8,128,1]{1,2,0:T(1,128)}), s32[8,128,1]{1,2,0:T(1,128)S(1)}, u32[]{:S(2)}, u32[]{:S(2)}) async-start(s32[8,128,1]{1,2,0:T(1,128)} %bitcast.5), calls=%async_computation | async-start | bytes 8192 | tf_op jit(solution)/shard_map/all_to_all | solution.py:43
  17.5 0.0 copy-done.1
  17.5 3.8 %scatter_custom_fusion.1 = bf16[1024,768]{1,0:T(8,128)(2,1)} fusion(s32[512]{0:T(512)S(1)} %compare_select_fusion, bf16[512,768]{1,0:T(8,128)(2,1)S(1)} %copy-done.1, bf16[]{:T(256)} %constant.105.clone.1), kind=kCustom, calls=%fused_computation.14 | custom fusion | bytes 1572866 | tf_op jit(solution)/shard_map/scatter | solution.py:17
  21.3 0.7 all-to-all-done
  22.0 4.2 %all-to-all-start.1 = ((bf16[8,128,768]{2,1,0:T(8,128)(2,1)}), bf16[8,128,768]{2,1,0:T(8,128)(2,1)S(1)}, u32[]{:S(2)}, u32[]{:S(2)}) async-start(bf16[8,128,768]{2,1,0:T(8,128)(2,1)} %bitcast.14), calls=%async_computation.1 | async-start | bytes 3145728 | tf_op jit(solution)/shard_map/all_to_all | solution.py:42
  26.1 0.0 reduce-scatter.4.cloned.1.call-start
  26.2 20.7 %all-to-all-done.1 = bf16[8,128,768]{2,1,0:T(8,128)(2,1)S(1)} async-done(((bf16[8,128,768]{2,1,0:T(8,128)(2,1)}), bf16[8,128,768]{2,1,0:T(8,128)(2,1)S(1)}, u32[]{:S(2)}, u32[]{:S(2)}) %all-to-all-start.1) | async-done | bytes 1572896 | tf_op jit(solution)/shard_map/all_to_all | solution.py:42
  46.9 13.4 %fusion = f32[6272,768]{1,0:T(8,128)} fusion(bf16[1024,768]{1,0:T(8,128)(2,1)S(1)} %bitcast.53, s32[1024]{0:T(1024)S(1)} %get-tuple-element.3, s32[1024]{0:T(1024)S(1)} %get-tuple-element.2), kind=kOutput, calls=%fused_computation.7 | convolution fusion | flops 9884270592 | bytes 20848640 | tf_op jit(solution)/shard_map/dot_general | solution.py:52
  60.2 0.0 reduce-scatter.4.cloned.1.call-update
  60.2 0.0 all-gather.2.cloned.1.call-start
  60.3 124.5 %reduce-scatter.4.cloned.1.call-done = f32[392,768]{1,0:T(8,128)} async-done(((f32[6272,768]{1,0:T(8,128)}), f32[392,768]{1,0:T(8,128)}) %reduce-scatter.4.cloned.1.call-update) | async-done | bytes 1204240
  184.8 0.0 copy-start
  184.8 1.5 multiply_reduce_fusion.1
  186.4 0.1 copy-done
  186.5 0.9 multiply_convert_fusion
  187.4 0.0 all-gather.2.cloned.1.call-update
  187.5 0.2 multiply_reduce_fusion
  187.7 76.4 %all-gather.2.cloned.1.call-done = bf16[6272,768]{1,0:T(8,128)(2,1)} async-done(((bf16[392,768]{1,0:T(8,128)(2,1)}), bf16[6272,768]{1,0:T(8,128)(2,1)}) %all-gather.2.cloned.1.call-update) | async-done | bytes 9633808 | tf_op jit(solution)/shard_map/all_gather | solution.py:58
  264.1 16.0 %select_reduce_fusion = f32[1024]{0:T(1024)} fusion(bf16[1024,768]{1,0:T(8,128)(2,1)S(1)} %bitcast.54, bf16[6272,768]{1,0:T(8,128)(2,1)} %all-gather.2.cloned.1.call-done, s32[1024]{0:T(1024)S(1)} %get-tuple-element.2), kind=kOutput, calls=%fused_computation.3 | convolution fusion | flops 9884269568 | bytes 11214848 | tf_op jit(solution)/shard_map/dot_general | solution.py:59
  280.1 4.9 %all-to-all-start.2 = ((f32[8,128,1]{1,2,0:T(1,128)}), f32[8,128,1]{1,2,0:T(1,128)S(1)}, u32[]{:S(2)}, u32[]{:S(2)}) async-start(f32[8,128,1]{1,2,0:T(1,128)} %bitcast.17), calls=%async_computation.2 | async-start | bytes 8192 | tf_op jit(solution)/shard_map/all_to_all | solution.py:63
  285.0 4.6 %all-to-all-done.2 = f32[8,128,1]{1,2,0:T(1,128)S(1)} async-done(((f32[8,128,1]{1,2,0:T(1,128)}), f32[8,128,1]{1,2,0:T(1,128)S(1)}, u32[]{:S(2)}, u32[]{:S(2)}) %all-to-all-start.2) | async-done | bytes 4128 | tf_op jit(solution)/shard_map/all_to_all | solution.py:63
  289.6 2.3 gather_fusion
  291.8 0.6 multiply_multiply_fusion
  (10 shorter events, 0.1 us)
Async XLA Ops:
  7.2 10.3 %copy-start.1 = (bf16[512,768]{1,0:T(8,128)(2,1)S(1)}, bf16[512,768]{1,0:T(8,128)(2,1)}, u32[]{:S(2)}) copy-start(bf16[512,768]{1,0:T(8,128)(2,1)} %param.3) | copy-start | bytes 2359300
  11.7 10.3 %all-to-all-start = ((s32[8,128,1]{1,2,0:T(1,128)}), s32[8,128,1]{1,2,0:T(1,128)S(1)}, u32[]{:S(2)}, u32[]{:S(2)}) async-start(s32[8,128,1]{1,2,0:T(1,128)} %bitcast.5), calls=%async_computation | async-start | bytes 8192 | tf_op jit(solution)/shard_map/all_to_all | solution.py:43
  22.0 24.9 %all-to-all-start.1 = ((bf16[8,128,768]{2,1,0:T(8,128)(2,1)}), bf16[8,128,768]{2,1,0:T(8,128)(2,1)S(1)}, u32[]{:S(2)}, u32[]{:S(2)}) async-start(bf16[8,128,768]{2,1,0:T(8,128)(2,1)} %bitcast.14), calls=%async_computation.1 | async-start | bytes 3145728 | tf_op jit(solution)/shard_map/all_to_all | solution.py:42
  26.1 158.7 %reduce-scatter.4.cloned.1.call-start = ((), (), s32[]{:S(2)}) async-start(), calls=%async_computation.5 | async-start | bytes 20471808
  60.2 203.9 %all-gather.2.cloned.1.call-start = ((), (), s32[]{:S(2)}) async-start(), calls=%async_computation.4 | async-start | bytes 10235904 | tf_op jit(solution)/shard_map/all_gather | solution.py:58
  184.8 1.6 copy-start
  280.1 9.5 %all-to-all-start.2 = ((f32[8,128,1]{1,2,0:T(1,128)}), f32[8,128,1]{1,2,0:T(1,128)S(1)}, u32[]{:S(2)}, u32[]{:S(2)}) async-start(f32[8,128,1]{1,2,0:T(1,128)} %bitcast.17), calls=%async_computation.2 | async-start | bytes 8192 | tf_op jit(solution)/shard_map/all_to_all | solution.py:63
Sparse Core Ops, SparseCore 0:
  60.4 124.4 reduce-scatter.3
  187.8 76.2 all-gather.1
where the time goes:
time: 300 us; the launch traced here: 299 us
  waiting for transfers between devices  227 us (76%)
  matrix products  29.3 us (10%)
  starting transfers between devices  14.9 us (5%)
  between operations  14.1 us (5%)
  local copies, waits for them, and re-layouts  9.33 us (3%)
  other arithmetic  4.63 us (2%)
    unnamed x3, waiting for transfers between devices  125 us
    all_gather x1, waiting for transfers between devices, body(): piece = lax.all_gather(centroids, 'doc', axis=0, tiled=True)  76.4 us
    all_to_all x1, waiting for transfers between devices, body(): lax.all_to_all(outgoing, 'own', split_axis=0, concat_axis=0, tiled=True)  20.7 us
    dot_general x1, matrix products, body(): similar = jnp.dot(arrived, piece.T, preferred_element_type=jnp.float32)  16 us
    dot_general x1, matrix products, body(): jnp.dot(table, arrived, preferred_element_type=jnp.float32)  13.4 us
  transfers between devices with their start and end apart: 5, of which 5 were waited for; matrix products, arithmetic and copies ran while one was open for 1% of the time, Pallas kernels for 0%

commit v1 on v0

--- a/solution.py
+++ b/solution.py
@@ -55,7 +55,12 @@
         tiled=True,
     )
     centroids = unit_rows(sums, width)
-    piece = lax.all_gather(centroids, "doc", axis=0, tiled=True)
+    ring = [centroids]
+    for hop in range(15):
+        ring.append(lax.ppermute(ring[-1], "doc", [(dev, (dev + 1) % 16) for dev in range(16)]))
+    piece = jnp.roll(
+        jnp.concatenate(ring[::-1], axis=0), (lax.axis_index("doc") + 1) * ring[0].shape[0], axis=0
+    )
     similar = jnp.dot(arrived, piece.T, preferred_element_type=jnp.float32)
     column = owner_index - jnp.int32(0)
     chosen = column[:, None] == jnp.arange(piece.shape[0], dtype=jnp.int32)[None, :]

time: 300 us -> 526 us (1.75)
  waiting for transfers between devices: 227 us -> 378 us
  local copies, waits for them, and re-layouts: 9.33 us -> 59.5 us
  starting transfers between devices: 14.9 us -> 32.4 us
    ppermute x0 -> x15, waiting for transfers between devices: none -> 228 us  [body(): lax.ppermute(ring[-1], 'doc', [(dev, (dev + 1) % 16) for dev in range(16)])]
    all_gather x1 -> x0, waiting for transfers between devices: 76.4 us -> none  [body(): piece = lax.all_gather(centroids, 'doc', axis=0, tiled=True)]
    unnamed x5 -> x79, local copies, waits for them, and re-layouts: 0.1 us -> 49.7 us
    all_to_all x1, starting transfers between devices: 4.92 us -> 20.6 us  [body(): lax.all_to_all(products, 'own', split_axis=0, concat_axis=0, tiled=True)]
    unnamed x3 -> x2, waiting for transfers between devices: 125 us -> 124 us
  transfers between devices with their start and end apart: 5 -> 19, of which waited for: 5 -> 19; matrix products, arithmetic and copies ran while one was open for 1% -> 1% of each run, Pallas kernels for 0% -> 0%
where the time goes in v1:
time: 526 us; the launch traced here: 525 us
  waiting for transfers between devices  378 us (72%)
  local copies, waits for them, and re-layouts  59.5 us (11%)
  matrix products  33 us (6%)
  starting transfers between devices  32.4 us (6%)
  between operations  14.2 us (3%)
  other arithmetic  8.21 us (2%)
    ppermute x15, waiting for transfers between devices, body(): lax.ppermute(ring[-1], 'doc', [(dev, (dev + 1) % 16) for dev in range(16)])  228 us
    unnamed x2, waiting for transfers between devices  124 us
    unnamed x79, local copies, waits for them, and re-layouts  49.7 us
    all_to_all x1, waiting for transfers between devices, body(): lax.all_to_all(outgoing, 'own', split_axis=0, concat_axis=0, tiled=True)  20.7 us
    all_to_all x1, starting transfers between devices, body(): lax.all_to_all(products, 'own', split_axis=0, concat_axis=0, tiled=True)  20.6 us
    dot_general x1, matrix products, body(): similar = jnp.dot(arrived, piece.T, preferred_element_type=jnp.float32)  19.7 us
    dot_general x1, matrix products, body(): jnp.dot(table, arrived, preferred_element_type=jnp.float32)  13.3 us
  transfers between devices with their start and end apart: 19, of which 19 were waited for; matrix products, arithmetic and copies ran while one was open for 1% of the time, Pallas kernels for 0%

profile of v1, /device:TPU:1, one launch (start us, length us, event | category | flops | bytes accessed | tf_op | source)
XLA Modules:
  0.0 525.1 jit_solution(6474274193660067909)
XLA Ops:
  8.6 3.0 scatter_custom_fusion
  11.6 5.8 %all-to-all-start = ((s32[8,128,1]{1,2,0:T(1,128)}), s32[8,128,1]{1,2,0:T(1,128)S(1)}, u32[]{:S(2)}, u32[]{:S(2)}) async-start(s32[8,128,1]{1,2,0:T(1,128)} %bitcast.5), calls=%async_computation | async-start | bytes 8192 | tf_op jit(solution)/shard_map/all_to_all | solution.py:43
  17.4 4.4 scatter_custom_fusion.1
  21.9 4.7 all-to-all-start.1
  26.6 20.7 %all-to-all-done.1 = bf16[8,128,768]{2,1,0:T(8,128)(2,1)S(1)} async-done(((bf16[8,128,768]{2,1,0:T(8,128)(2,1)}), bf16[8,128,768]{2,1,0:T(8,128)(2,1)S(1)}, u32[]{:S(2)}, u32[]{:S(2)}) %all-to-all-start.1) | async-done | bytes 1572896 | tf_op jit(solution)/shard_map/all_to_all | solution.py:42
  47.3 13.3 %fusion = f32[6272,768]{1,0:T(8,128)} fusion(bf16[1024,768]{1,0:T(8,128)(2,1)S(1)} %bitcast.52, s32[1024]{0:T(1024)S(1)} %get-tuple-element.3, s32[1024]{0:T(1024)S(1)} %get-tuple-element.2), kind=kOutput, calls=%fused_computation.7 | convolution fusion | flops 9884270592 | bytes 20848640 | tf_op jit(solution)/shard_map/dot_general | solution.py:52
  60.6 124.5 %reduce-scatter.4.cloned.1.call-done = f32[392,768]{1,0:T(8,128)} async-done(((f32[6272,768]{1,0:T(8,128)}), f32[392,768]{1,0:T(8,128)}) %reduce-scatter.4.cloned.1.call-update) | async-done | bytes 1204240
  185.1 1.5 multiply_reduce_fusion.1
  186.7 1.4 multiply_convert_fusion
  188.1 1.2 collective-permute-start
  189.4 16.5 %collective-permute-done = bf16[392,768]{1,0:T(8,128)(2,1)S(1)} collective-permute-done((bf16[392,768]{1,0:T(8,128)(2,1)S(1)}, bf16[392,768]{1,0:T(8,128)(2,1)S(1)}, u32[]{:S(2)}, u32[]{:S(2)}) %collective-permute-start) | collective-permute-done | bytes 602144 | tf_op jit(solution)/shard_map/ppermute | solution.py:60
  205.9 16.8 %collective-permute-done.1 = bf16[392,768]{1,0:T(8,128)(2,1)S(1)} collective-permute-done((bf16[392,768]{1,0:T(8,128)(2,1)S(1)}, bf16[392,768]{1,0:T(8,128)(2,1)S(1)}, u32[]{:S(2)}, u32[]{:S(2)}) %collective-permute-start.1) | collective-permute-done | bytes 602144 | tf_op jit(solution)/shard_map/ppermute | solution.py:60
  222.7 15.9 %collective-permute-done.2 = bf16[392,768]{1,0:T(8,128)(2,1)S(1)} collective-permute-done((bf16[392,768]{1,0:T(8,128)(2,1)S(1)}, bf16[392,768]{1,0:T(8,128)(2,1)S(1)}, u32[]{:S(2)}, u32[]{:S(2)}) %collective-permute-start.2) | collective-permute-done | bytes 602144 | tf_op jit(solution)/shard_map/ppermute | solution.py:60
  238.6 14.9 %collective-permute-done.3 = bf16[392,768]{1,0:T(8,128)(2,1)S(1)} collective-permute-done((bf16[392,768]{1,0:T(8,128)(2,1)S(1)}, bf16[392,768]{1,0:T(8,128)(2,1)S(1)}, u32[]{:S(2)}, u32[]{:S(2)}) %collective-permute-start.3) | collective-permute-done | bytes 602144 | tf_op jit(solution)/shard_map/ppermute | solution.py:60
  254.3 14.0 %collective-permute-done.4 = bf16[392,768]{1,0:T(8,128)(2,1)S(1)} collective-permute-done((bf16[392,768]{1,0:T(8,128)(2,1)S(1)}, bf16[392,768]{1,0:T(8,128)(2,1)S(1)}, u32[]{:S(2)}, u32[]{:S(2)}) %collective-permute-start.4) | collective-permute-done | bytes 602144 | tf_op jit(solution)/shard_map/ppermute | solution.py:60
  269.2 13.1 %collective-permute-done.5 = bf16[392,768]{1,0:T(8,128)(2,1)S(1)} collective-permute-done((bf16[392,768]{1,0:T(8,128)(2,1)S(1)}, bf16[392,768]{1,0:T(8,128)(2,1)S(1)}, u32[]{:S(2)}, u32[]{:S(2)}) %collective-permute-start.5) | collective-permute-done | bytes 602144 | tf_op jit(solution)/shard_map/ppermute | solution.py:60
  283.1 12.2 %collective-permute-done.6 = bf16[392,768]{1,0:T(8,128)(2,1)S(1)} collective-permute-done((bf16[392,768]{1,0:T(8,128)(2,1)S(1)}, bf16[392,768]{1,0:T(8,128)(2,1)S(1)}, u32[]{:S(2)}, u32[]{:S(2)}) %collective-permute-start.6) | collective-permute-done | bytes 602144 | tf_op jit(solution)/shard_map/ppermute | solution.py:60
  296.1 12.3 %collective-permute-done.7 = bf16[392,768]{1,0:T(8,128)(2,1)S(1)} collective-permute-done((bf16[392,768]{1,0:T(8,128)(2,1)S(1)}, bf16[392,768]{1,0:T(8,128)(2,1)S(1)}, u32[]{:S(2)}, u32[]{:S(2)}) %collective-permute-start.7) | collective-permute-done | bytes 602144 | tf_op jit(solution)/shard_map/ppermute | solution.py:60
  309.3 13.3 %collective-permute-done.8 = bf16[392,768]{1,0:T(8,128)(2,1)S(1)} collective-permute-done((bf16[392,768]{1,0:T(8,128)(2,1)S(1)}, bf16[392,768]{1,0:T(8,128)(2,1)S(1)}, u32[]{:S(2)}, u32[]{:S(2)}) %collective-permute-start.8) | collective-permute-done | bytes 602144 | tf_op jit(solution)/shard_map/ppermute | solution.py:60
  323.6 14.4 %collective-permute-done.9 = bf16[392,768]{1,0:T(8,128)(2,1)S(1)} collective-permute-done((bf16[392,768]{1,0:T(8,128)(2,1)S(1)}, bf16[392,768]{1,0:T(8,128)(2,1)S(1)}, u32[]{:S(2)}, u32[]{:S(2)}) %collective-permute-start.9) | collective-permute-done | bytes 602144 | tf_op jit(solution)/shard_map/ppermute | solution.py:60
  338.8 15.6 %collective-permute-done.10 = bf16[392,768]{1,0:T(8,128)(2,1)S(1)} collective-permute-done((bf16[392,768]{1,0:T(8,128)(2,1)S(1)}, bf16[392,768]{1,0:T(8,128)(2,1)S(1)}, u32[]{:S(2)}, u32[]{:S(2)}) %collective-permute-start.10) | collective-permute-done | bytes 602144 | tf_op jit(solution)/shard_map/ppermute | solution.py:60
  355.1 16.6 %collective-permute-done.11 = bf16[392,768]{1,0:T(8,128)(2,1)S(1)} collective-permute-done((bf16[392,768]{1,0:T(8,128)(2,1)S(1)}, bf16[392,768]{1,0:T(8,128)(2,1)S(1)}, u32[]{:S(2)}, u32[]{:S(2)}) %collective-permute-start.11) | collective-permute-done | bytes 602144 | tf_op jit(solution)/shard_map/ppermute | solution.py:60
  372.6 17.7 %collective-permute-done.12 = bf16[392,768]{1,0:T(8,128)(2,1)S(1)} collective-permute-done((bf16[392,768]{1,0:T(8,128)(2,1)S(1)}, bf16[392,768]{1,0:T(8,128)(2,1)S(1)}, u32[]{:S(2)}, u32[]{:S(2)}) %collective-permute-start.12) | collective-permute-done | bytes 602144 | tf_op jit(solution)/shard_map/ppermute | solution.py:60
  391.2 18.7 %collective-permute-done.13 = bf16[392,768]{1,0:T(8,128)(2,1)} collective-permute-done((bf16[392,768]{1,0:T(8,128)(2,1)S(1)}, bf16[392,768]{1,0:T(8,128)(2,1)}, u32[]{:S(2)}, u32[]{:S(2)}) %collective-permute-start.13) | collective-permute-done | bytes 602144 | tf_op jit(solution)/shard_map/ppermute | solution.py:60
  410.0 1.5 multiply_reduce_fusion
  411.5 15.9 %collective-permute-done.14 = bf16[392,768]{1,0:T(8,128)(2,1)} collective-permute-done((bf16[392,768]{1,0:T(8,128)(2,1)}, bf16[392,768]{1,0:T(8,128)(2,1)}, u32[]{:S(2)}, u32[]{:S(2)}) %collective-permute-start.14) | collective-permute-done | bytes 602144 | tf_op jit(solution)/shard_map/ppermute | solution.py:60
  427.3 1.9 constant_dynamic-update-slice_fusion.31
  429.3 2.1 constant_dynamic-update-slice_fusion.30
  431.3 1.9 constant_dynamic-update-slice_fusion.29
  433.3 1.9 constant_dynamic-update-slice_fusion.28
  435.2 1.9 constant_dynamic-update-slice_fusion.27
  437.1 1.9 constant_dynamic-update-slice_fusion.26
  439.1 1.9 constant_dynamic-update-slice_fusion.25
  441.0 1.9 constant_dynamic-update-slice_fusion.24
  442.9 1.9 constant_dynamic-update-slice_fusion.23
  444.9 1.9 constant_dynamic-update-slice_fusion.22
  446.8 1.9 constant_dynamic-update-slice_fusion.21
  448.7 1.9 constant_dynamic-update-slice_fusion.20
  451.5 0.9 constant_dynamic-update-slice_fusion.18
  452.4 0.9 constant_dynamic-update-slice_fusion.17
  453.4 0.9 constant_dynamic-update-slice_fusion.16
  454.3 1.9 constant_dynamic-update-slice_fusion.15
  456.2 1.9 constant_dynamic-update-slice_fusion.14
  469.6 1.0 constant_dynamic-update-slice_fusion
  470.5 19.7 %select_reduce_fusion = f32[1024]{0:T(1024)} fusion(bf16[1024,768]{1,0:T(8,128)(2,1)S(1)} %bitcast.53, s32[1024]{0:T(1024)S(1)} %get-tuple-element.2, bf16[12544,768]{1,0:T(8,128)(2,1)} %constant_dynamic-update-slice_fusion, s32[]{:T(128)S(6)} %select_n.117), kind=kOutput, calls=%fused_computation.3 | convolution fusion | flops 9884269568 | bytes 11214852 | tf_op jit(solution)/shard_map/dot_general | solution.py:64
  490.2 20.6 %all-to-all-start.2 = ((f32[8,128,1]{1,2,0:T(1,128)}), f32[8,128,1]{1,2,0:T(1,128)S(1)}, u32[]{:S(2)}, u32[]{:S(2)}) async-start(f32[8,128,1]{1,2,0:T(1,128)} %bitcast.17), calls=%async_computation.2 | async-start | bytes 8192 | tf_op jit(solution)/shard_map/all_to_all | solution.py:68
  510.8 4.6 all-to-all-done.2
  515.4 2.3 gather_fusion
  (94 shorter events, 22.8 us)
Async XLA Ops:
  11.6 10.3 %all-to-all-start = ((s32[8,128,1]{1,2,0:T(1,128)}), s32[8,128,1]{1,2,0:T(1,128)S(1)}, u32[]{:S(2)}, u32[]{:S(2)}) async-start(s32[8,128,1]{1,2,0:T(1,128)} %bitcast.5), calls=%async_computation | async-start | bytes 8192 | tf_op jit(solution)/shard_map/all_to_all | solution.py:43
  21.9 25.4 %all-to-all-start.1 = ((bf16[8,128,768]{2,1,0:T(8,128)(2,1)}), bf16[8,128,768]{2,1,0:T(8,128)(2,1)S(1)}, u32[]{:S(2)}, u32[]{:S(2)}) async-start(bf16[8,128,768]{2,1,0:T(8,128)(2,1)} %bitcast.14), calls=%async_computation.1 | async-start | bytes 3145728 | tf_op jit(solution)/shard_map/all_to_all | solution.py:42
  26.6 158.5 %reduce-scatter.4.cloned.1.call-start = ((), (), s32[]{:S(2)}) async-start(), calls=%async_computation.4 | async-start | bytes 20471808
  47.3 13.3 %copy-start.21 = (bf16[8,128,768]{2,1,0:T(8,128)(2,1)}, bf16[8,128,768]{2,1,0:T(8,128)(2,1)S(1)}, u32[]{:S(2)}) copy-start(bf16[8,128,768]{2,1,0:T(8,128)(2,1)S(1)} %all-to-all-done.1) | copy-start | bytes 4718596
  185.1 268.3 %copy-start = (f32[392,768]{1,0:T(8,128)S(1)}, f32[392,768]{1,0:T(8,128)}, u32[]{:S(2)}) copy-start(f32[392,768]{1,0:T(8,128)} %reduce-scatter.4.cloned.1.call-done) | copy-start | bytes 3612676
  188.1 221.8 %copy-start.23 = (bf16[392,768]{1,0:T(8,128)(2,1)}, bf16[392,768]{1,0:T(8,128)(2,1)S(1)}, u32[]{:S(2)}) copy-start(bf16[392,768]{1,0:T(8,128)(2,1)S(1)} %multiply_convert_fusion) | copy-start | bytes 1806340
  188.1 17.8 %collective-permute-start = (bf16[392,768]{1,0:T(8,128)(2,1)S(1)}, bf16[392,768]{1,0:T(8,128)(2,1)S(1)}, u32[]{:S(2)}, u32[]{:S(2)}) collective-permute-start(bf16[392,768]{1,0:T(8,128)(2,1)S(1)} %multiply_convert_fusion), channel_id=1, source_target_pairs={{0,8},{8,16},{16,24},{24,32},{32,40},{40,48},{48,56},{56,64},{64,7... | collective-permute-start | bytes 1806344 | tf_op jit(solution)/shard_map/ppermute | solution.py:60
  205.9 16.8 %collective-permute-start.1 = (bf16[392,768]{1,0:T(8,128)(2,1)S(1)}, bf16[392,768]{1,0:T(8,128)(2,1)S(1)}, u32[]{:S(2)}, u32[]{:S(2)}) collective-permute-start(bf16[392,768]{1,0:T(8,128)(2,1)S(1)} %collective-permute-done), channel_id=1, source_target_pairs={{0,8},{8,16},{16,24},{24,32},{32,40},{40,48},{48,56},{56,64},{64,7... | collective-permute-start | bytes 1806344 | tf_op jit(solution)/shard_map/ppermute | solution.py:60
  222.7 15.9 %collective-permute-start.2 = (bf16[392,768]{1,0:T(8,128)(2,1)S(1)}, bf16[392,768]{1,0:T(8,128)(2,1)S(1)}, u32[]{:S(2)}, u32[]{:S(2)}) collective-permute-start(bf16[392,768]{1,0:T(8,128)(2,1)S(1)} %collective-permute-done.1), channel_id=1, source_target_pairs={{0,8},{8,16},{16,24},{24,32},{32,40},{40,48},{48,56},{56,64},{64,7... | collective-permute-start | bytes 1806344 | tf_op jit(solution)/shard_map/ppermute | solution.py:60
  238.6 14.9 %collective-permute-start.3 = (bf16[392,768]{1,0:T(8,128)(2,1)S(1)}, bf16[392,768]{1,0:T(8,128)(2,1)S(1)}, u32[]{:S(2)}, u32[]{:S(2)}) collective-permute-start(bf16[392,768]{1,0:T(8,128)(2,1)S(1)} %collective-permute-done.2), channel_id=1, source_target_pairs={{0,8},{8,16},{16,24},{24,32},{32,40},{40,48},{48,56},{56,64},{64,7... | collective-permute-start | bytes 1806344 | tf_op jit(solution)/shard_map/ppermute | solution.py:60
  253.5 0.8 copy-start.1
  254.3 14.0 %collective-permute-start.4 = (bf16[392,768]{1,0:T(8,128)(2,1)S(1)}, bf16[392,768]{1,0:T(8,128)(2,1)S(1)}, u32[]{:S(2)}, u32[]{:S(2)}) collective-permute-start(bf16[392,768]{1,0:T(8,128)(2,1)S(1)} %collective-permute-done.3), channel_id=1, source_target_pairs={{0,8},{8,16},{16,24},{24,32},{32,40},{40,48},{48,56},{56,64},{64,7... | collective-permute-start | bytes 1806344 | tf_op jit(solution)/shard_map/ppermute | solution.py:60
  268.4 0.8 copy-start.3
  269.2 13.1 %collective-permute-start.5 = (bf16[392,768]{1,0:T(8,128)(2,1)S(1)}, bf16[392,768]{1,0:T(8,128)(2,1)S(1)}, u32[]{:S(2)}, u32[]{:S(2)}) collective-permute-start(bf16[392,768]{1,0:T(8,128)(2,1)S(1)} %collective-permute-done.4), channel_id=1, source_target_pairs={{0,8},{8,16},{16,24},{24,32},{32,40},{40,48},{48,56},{56,64},{64,7... | collective-permute-start | bytes 1806344 | tf_op jit(solution)/shard_map/ppermute | solution.py:60
  282.3 0.8 copy-start.5
  283.1 12.2 %collective-permute-start.6 = (bf16[392,768]{1,0:T(8,128)(2,1)S(1)}, bf16[392,768]{1,0:T(8,128)(2,1)S(1)}, u32[]{:S(2)}, u32[]{:S(2)}) collective-permute-start(bf16[392,768]{1,0:T(8,128)(2,1)S(1)} %collective-permute-done.5), channel_id=1, source_target_pairs={{0,8},{8,16},{16,24},{24,32},{32,40},{40,48},{48,56},{56,64},{64,7... | collective-permute-start | bytes 1806344 | tf_op jit(solution)/shard_map/ppermute | solution.py:60
  295.3 0.8 copy-start.7
  296.1 12.3 %collective-permute-start.7 = (bf16[392,768]{1,0:T(8,128)(2,1)S(1)}, bf16[392,768]{1,0:T(8,128)(2,1)S(1)}, u32[]{:S(2)}, u32[]{:S(2)}) collective-permute-start(bf16[392,768]{1,0:T(8,128)(2,1)S(1)} %collective-permute-done.6), channel_id=1, source_target_pairs={{0,8},{8,16},{16,24},{24,32},{32,40},{40,48},{48,56},{56,64},{64,7... | collective-permute-start | bytes 1806344 | tf_op jit(solution)/shard_map/ppermute | solution.py:60
  308.4 0.9 copy-start.9
  309.3 13.4 %collective-permute-start.8 = (bf16[392,768]{1,0:T(8,128)(2,1)S(1)}, bf16[392,768]{1,0:T(8,128)(2,1)S(1)}, u32[]{:S(2)}, u32[]{:S(2)}) collective-permute-start(bf16[392,768]{1,0:T(8,128)(2,1)S(1)} %collective-permute-done.7), channel_id=1, source_target_pairs={{0,8},{8,16},{16,24},{24,32},{32,40},{40,48},{48,56},{56,64},{64,7... | collective-permute-start | bytes 1806344 | tf_op jit(solution)/shard_map/ppermute | solution.py:60
  322.7 0.9 copy-start.11
  323.6 14.4 %collective-permute-start.9 = (bf16[392,768]{1,0:T(8,128)(2,1)S(1)}, bf16[392,768]{1,0:T(8,128)(2,1)S(1)}, u32[]{:S(2)}, u32[]{:S(2)}) collective-permute-start(bf16[392,768]{1,0:T(8,128)(2,1)S(1)} %collective-permute-done.8), channel_id=1, source_target_pairs={{0,8},{8,16},{16,24},{24,32},{32,40},{40,48},{48,56},{56,64},{64,7... | collective-permute-start | bytes 1806344 | tf_op jit(solution)/shard_map/ppermute | solution.py:60
  338.0 0.8 copy-start.13
  338.8 15.6 %collective-permute-start.10 = (bf16[392,768]{1,0:T(8,128)(2,1)S(1)}, bf16[392,768]{1,0:T(8,128)(2,1)S(1)}, u32[]{:S(2)}, u32[]{:S(2)}) collective-permute-start(bf16[392,768]{1,0:T(8,128)(2,1)S(1)} %collective-permute-done.9), channel_id=1, source_target_pairs={{0,8},{8,16},{16,24},{24,32},{32,40},{40,48},{48,56},{56,64},{64,7... | collective-permute-start | bytes 1806344 | tf_op jit(solution)/shard_map/ppermute | solution.py:60
  354.3 0.8 copy-start.15
  355.1 16.6 %collective-permute-start.11 = (bf16[392,768]{1,0:T(8,128)(2,1)S(1)}, bf16[392,768]{1,0:T(8,128)(2,1)S(1)}, u32[]{:S(2)}, u32[]{:S(2)}) collective-permute-start(bf16[392,768]{1,0:T(8,128)(2,1)S(1)} %collective-permute-done.10), channel_id=1, source_target_pairs={{0,8},{8,16},{16,24},{24,32},{32,40},{40,48},{48,56},{56,64},{64,7... | collective-permute-start | bytes 1806344 | tf_op jit(solution)/shard_map/ppermute | solution.py:60
  371.8 0.8 copy-start.17
  372.6 17.7 %collective-permute-start.12 = (bf16[392,768]{1,0:T(8,128)(2,1)S(1)}, bf16[392,768]{1,0:T(8,128)(2,1)S(1)}, u32[]{:S(2)}, u32[]{:S(2)}) collective-permute-start(bf16[392,768]{1,0:T(8,128)(2,1)S(1)} %collective-permute-done.11), channel_id=1, source_target_pairs={{0,8},{8,16},{16,24},{24,32},{32,40},{40,48},{48,56},{56,64},{64,7... | collective-permute-start | bytes 1806344 | tf_op jit(solution)/shard_map/ppermute | solution.py:60
  390.3 0.8 copy-start.19
  391.1 18.7 %collective-permute-start.13 = (bf16[392,768]{1,0:T(8,128)(2,1)S(1)}, bf16[392,768]{1,0:T(8,128)(2,1)}, u32[]{:S(2)}, u32[]{:S(2)}) collective-permute-start(bf16[392,768]{1,0:T(8,128)(2,1)S(1)} %collective-permute-done.12), channel_id=1, source_target_pairs={{0,8},{8,16},{16,24},{24,32},{32,40},{40,48},{48,56},{56,64},{64,7... | collective-permute-start | bytes 1806344 | tf_op jit(solution)/shard_map/ppermute | solution.py:60
  409.9 17.5 %collective-permute-start.14 = (bf16[392,768]{1,0:T(8,128)(2,1)}, bf16[392,768]{1,0:T(8,128)(2,1)}, u32[]{:S(2)}, u32[]{:S(2)}) collective-permute-start(bf16[392,768]{1,0:T(8,128)(2,1)} %collective-permute-done.13), channel_id=1, source_target_pairs={{0,8},{8,16},{16,24},{24,32},{32,40},{40,48},{48,56},{56,64},{64,7... | collective-permute-start | bytes 1806344 | tf_op jit(solution)/shard_map/ppermute | solution.py:60
  409.9 48.3 %copy-start.20 = (bf16[392,768]{1,0:T(8,128)(2,1)S(1)}, bf16[392,768]{1,0:T(8,128)(2,1)}, u32[]{:S(2)}) copy-start(bf16[392,768]{1,0:T(8,128)(2,1)} %copy-done.19) | copy-start | bytes 1806340
  409.9 49.2 %copy-start.18 = (bf16[392,768]{1,0:T(8,128)(2,1)S(1)}, bf16[392,768]{1,0:T(8,128)(2,1)}, u32[]{:S(2)}) copy-start(bf16[392,768]{1,0:T(8,128)(2,1)} %copy-done.17) | copy-start | bytes 1806340
  409.9 50.0 %copy-start.16 = (bf16[392,768]{1,0:T(8,128)(2,1)S(1)}, bf16[392,768]{1,0:T(8,128)(2,1)}, u32[]{:S(2)}) copy-start(bf16[392,768]{1,0:T(8,128)(2,1)} %copy-done.15) | copy-start | bytes 1806340
  409.9 50.9 %copy-start.14 = (bf16[392,768]{1,0:T(8,128)(2,1)S(1)}, bf16[392,768]{1,0:T(8,128)(2,1)}, u32[]{:S(2)}) copy-start(bf16[392,768]{1,0:T(8,128)(2,1)} %copy-done.13) | copy-start | bytes 1806340
  409.9 51.8 %copy-start.12 = (bf16[392,768]{1,0:T(8,128)(2,1)S(1)}, bf16[392,768]{1,0:T(8,128)(2,1)}, u32[]{:S(2)}) copy-start(bf16[392,768]{1,0:T(8,128)(2,1)} %copy-done.11) | copy-start | bytes 1806340
  409.9 52.7 %copy-start.10 = (bf16[392,768]{1,0:T(8,128)(2,1)S(1)}, bf16[392,768]{1,0:T(8,128)(2,1)}, u32[]{:S(2)}) copy-start(bf16[392,768]{1,0:T(8,128)(2,1)} %copy-done.9) | copy-start | bytes 1806340
  409.9 53.5 %copy-start.8 = (bf16[392,768]{1,0:T(8,128)(2,1)S(1)}, bf16[392,768]{1,0:T(8,128)(2,1)}, u32[]{:S(2)}) copy-start(bf16[392,768]{1,0:T(8,128)(2,1)} %copy-done.7) | copy-start | bytes 1806340
  409.9 54.4 %copy-start.6 = (bf16[392,768]{1,0:T(8,128)(2,1)S(1)}, bf16[392,768]{1,0:T(8,128)(2,1)}, u32[]{:S(2)}) copy-start(bf16[392,768]{1,0:T(8,128)(2,1)} %copy-done.5) | copy-start | bytes 1806340
  409.9 55.3 %copy-start.4 = (bf16[392,768]{1,0:T(8,128)(2,1)S(1)}, bf16[392,768]{1,0:T(8,128)(2,1)}, u32[]{:S(2)}) copy-start(bf16[392,768]{1,0:T(8,128)(2,1)} %copy-done.3) | copy-start | bytes 1806340
  409.9 56.1 %copy-start.2 = (bf16[392,768]{1,0:T(8,128)(2,1)S(1)}, bf16[392,768]{1,0:T(8,128)(2,1)}, u32[]{:S(2)}) copy-start(bf16[392,768]{1,0:T(8,128)(2,1)} %copy-done.1) | copy-start | bytes 1806340
  429.3 41.3 %copy-start.22 = (bf16[8,128,768]{2,1,0:T(8,128)(2,1)S(1)}, bf16[8,128,768]{2,1,0:T(8,128)(2,1)}, u32[]{:S(2)}) copy-start(bf16[8,128,768]{2,1,0:T(8,128)(2,1)} %copy-done.21) | copy-start | bytes 4718596
  490.2 25.2 %all-to-all-start.2 = ((f32[8,128,1]{1,2,0:T(1,128)}), f32[8,128,1]{1,2,0:T(1,128)S(1)}, u32[]{:S(2)}, u32[]{:S(2)}) async-start(f32[8,128,1]{1,2,0:T(1,128)} %bitcast.17), calls=%async_computation.2 | async-start | bytes 8192 | tf_op jit(solution)/shard_map/all_to_all | solution.py:68
Sparse Core Ops, SparseCore 0:
  60.8 124.3 reduce-scatter.3
